TPU v7x, 32 devices: a whole 2x2x4 slice. The times are simulated.
32 devices in a mesh: slab: 2 (over x), energy: 16 (over z, y, core).
Axes of the slice: x: 2, y: 2, z: 4, core: 2. Of those that a mesh axis runs over, the one named last changes fastest.
Arguments:
- retarded: bfloat16 [32, 3, 384, 384], P('energy', None, 'slab'), may hold values from -0.3125 to 0.3125
- injection: bfloat16 [32, 2, 384, 384], P('energy', None, 'slab'), may hold values from -6 to 6
- screened: bfloat16 [32, 2, 384, 384], P('energy', None, 'slab'), may hold values from -6 to 6
- pattern: int32 [384], P('slab'), may hold values from 0 to 1, as said below
Outputs:
- self_energy: bfloat16 [32, 2, 384, 384], P('energy', None, 'slab')
Inputs may be any that keep to these rules, and one draw needn't show every extreme that they name: `pattern`: exactly 128 of the 192 entries held by each index of slab are 1.
All inputs are finite; a program needn't handle non-finite values.
Results may differ from a plain program's by a relative error of at most 0.0058.
Values may be sent and summed in bfloat16 or wider, within the bound.
A program may use at most 64 MiB of HBM per device.

v0:
```python
import math

import jax
import jax.numpy as jnp
from jax import lax
from jax.sharding import PartitionSpec as P

B = 192


def with_halo(cells, sides, width):
    for axis, dim in sides:
        count = lax.axis_size(axis)
        ends = count - 1
        head = lax.slice_in_dim(cells, 0, width, axis=dim)
        tail = lax.slice_in_dim(cells, cells.shape[dim] - width, cells.shape[dim], axis=dim)
        cells = jnp.concatenate(
            [
                lax.ppermute(tail, axis, [(i, (i + 1) % count) for i in range(ends)]),
                cells,
                lax.ppermute(head, axis, [((i + 1) % count, i) for i in range(ends)]),
            ],
            axis=dim,
        )
    return cells


def stack_complex(blocks):
    half = blocks.shape[-1] // 2
    real_part = blocks[..., :half]
    imag_part = blocks[..., half:]
    upper = jnp.concatenate([real_part, imag_part], -1)
    lower = jnp.concatenate([-imag_part, real_part], -1)
    return jnp.concatenate([upper, lower], -2)


def split_table(table):
    high_part = lax.optimization_barrier(table.astype(jnp.bfloat16))
    low_part = (table - high_part.astype(jnp.float32)).astype(jnp.bfloat16)
    return (high_part, low_part)


def convolve(green, screen):
    count = green.shape[0]
    half = green.shape[-1] // 2
    energy_index = jnp.arange(count, dtype=jnp.int32)
    phase_angle = (
        2.0
        * math.pi
        / count
        * (energy_index[:, None] * energy_index[None, :] % count).astype(jnp.float32)
    )
    cosine_table = jnp.cos(phase_angle)
    sine_table = jnp.sin(phase_angle)
    cosine_high, cosine_low = split_table(cosine_table)
    sine_high, sine_low = split_table(sine_table)

    def apply_split(high_part, low_part, flat):
        first_pass = jnp.dot(high_part, flat, preferred_element_type=jnp.float32)
        return first_pass + jnp.dot(low_part, flat, preferred_element_type=jnp.float32)

    def forward(values):
        flat = values.reshape(count, -1)
        with_cos = apply_split(cosine_high, cosine_low, flat).reshape(values.shape)
        with_sin = apply_split(sine_high, sine_low, flat).reshape(values.shape)
        return (
            with_cos[..., :half] + with_sin[..., half:],
            with_cos[..., half:] - with_sin[..., :half],
        )

    green_real, green_imag = forward(green)
    screen_real, screen_imag = forward(screen)
    prod_real = green_real * screen_real - green_imag * screen_imag
    prod_imag = green_real * screen_imag + green_imag * screen_real
    values = jnp.concatenate([prod_real, prod_imag], -1)
    flat = values.reshape(count, -1)
    with_cos = jnp.dot(cosine_table, flat, precision=lax.Precision.HIGH).reshape(values.shape)
    with_sin = jnp.dot(sine_table, flat, precision=lax.Precision.HIGH).reshape(values.shape)
    with_cos, with_sin = (with_cos, with_sin)
    sigma_real = with_cos[..., :half] - with_sin[..., half:]
    sigma_imag = with_cos[..., half:] + with_sin[..., :half]
    factor = 1.0 / (count * math.sqrt(count))
    return jnp.concatenate([-sigma_imag, sigma_real], -1) * factor


def local(retarded, injection, screened, pattern):
    energy_count = retarded.shape[0]
    row_count = retarded.shape[2]
    block_count = row_count // B
    owners = lax.axis_size("energy")
    live_count = row_count * 2 // 3 // owners * owners
    live_order = jnp.argsort(1 - pattern, stable=True)[:live_count]
    screen_send = jnp.take(screened, live_order, axis=2)
    padded = with_halo(injection, (("slab", 2),), B)
    padded = padded.reshape(energy_count, 2, block_count + 2, B, 2 * B)
    row_blocks = retarded.reshape(energy_count, 3, block_count, B, 2 * B)
    total = jnp.zeros((energy_count, 2, block_count, B, 2 * B), jnp.float32)
    for offset in range(3):
        nearby = padded[:, :, offset : offset + block_count]
        expanded = stack_complex(nearby)
        row_block = row_blocks[:, offset]
        left_product = jnp.einsum(
            "enac,elncd->elnad", row_block, expanded, preferred_element_type=jnp.float32
        ).astype(jnp.bfloat16)
        swapped = jnp.concatenate([left_product[..., B:], -left_product[..., :B]], -1)
        real_part = jnp.einsum(
            "elnac,enbc->elnab", left_product, row_block, preferred_element_type=jnp.float32
        )
        imag_part = jnp.einsum(
            "elnac,enbc->elnab", swapped, row_block, preferred_element_type=jnp.float32
        )
        total = total + jnp.concatenate([real_part, imag_part], -1)
    green = total.astype(jnp.bfloat16).reshape(energy_count, 2, row_count, 2 * B)
    green_send = jnp.take(green, live_order, axis=2)
    green_owned, screen_owned = (
        lax.all_to_all(green_send, "energy", split_axis=2, concat_axis=0, tiled=True),
        lax.all_to_all(screen_send, "energy", split_axis=2, concat_axis=0, tiled=True),
    )
    sigma = convolve(green_owned, screen_owned).astype(jnp.bfloat16)
    returned_rows = lax.all_to_all(sigma, "energy", split_axis=0, concat_axis=2, tiled=True)
    result = jnp.zeros((energy_count, 2, row_count, 2 * B), jnp.bfloat16)
    result = result.at[:, :, live_order, :].set(returned_rows)
    return result


def solution(mesh):
    placed = (
        P("energy", None, "slab", None),
        P("energy", None, "slab", None),
        P("energy", None, "slab", None),
        P("slab"),
    )
    return jax.shard_map(
        local,
        mesh=mesh,
        in_specs=placed,
        out_specs=P("energy", None, "slab", None),
        check_vma=False,
    )
```

profile of v0, /device:TPU:0, one launch (start us, length us, event | category | flops | bytes accessed | tf_op | source)
XLA Modules:
  0.0 78.3 jit_solution(17833904391307359251)
XLA Ops:
  0.0 5.0 %collective-permute-start = (bf16[2,2,192,384]{3,2,1,0:T(8,128)(2,1)}, bf16[2,2,192,384]{3,2,1,0:T(8,128)(2,1)S(1)}, u32[]{:S(2)}, u32[]{:S(2)}) collective-permute-start(bf16[2,2,192,384]{3,2,1,0:T(8,128)(2,1)} %param.7), channel_id=1, source_target_pairs={{0,16},{1,17},{2,18},{3,19},{4,20},{5,21},{6,22},{7,23},{8,24},{9,... | collective-permute-start | bytes 1769480 | tf_op jit(solution)/shard_map/ppermute | solution.py:19
  5.0 1.3 %collective-permute-start.1 = (bf16[2,2,192,384]{3,2,1,0:T(8,128)(2,1)}, bf16[2,2,192,384]{3,2,1,0:T(8,128)(2,1)}, u32[]{:S(2)}, u32[]{:S(2)}) collective-permute-start(bf16[2,2,192,384]{3,2,1,0:T(8,128)(2,1)} %param.7), channel_id=1, source_target_pairs={{16,0},{17,1},{18,2},{19,3},{20,4},{21,5},{22,6},{23,7},{24,8},{25... | collective-permute-start | bytes 1769480 | tf_op jit(solution)/shard_map/ppermute | solution.py:21
  6.3 0.7 broadcast_subtract_fusion
  7.0 3.2 %sort.17 = (s32[192]{0:T(256)}, s32[192]{0:T(256)S(1)}) sort(s32[192]{0:T(256)S(1)} %broadcast_subtract_fusion, s32[192]{0:T(256)S(1)} %iota.11), dimensions={0}, to_apply=%region_0.0 | sort | flops 1536 | bytes 3072 | tf_op jit(solution)/shard_map/jit(argsort)/sort | solution.py:92
  10.2 1.9 %gather_fusion.1 = bf16[128,2,2,384]{3,0,2,1:T(8,128)(2,1)S(1)} fusion(bf16[2,2,192,384]{3,2,1,0:T(8,128)(2,1)S(1)} %copy-done, s32[1024]{0:T(1024)S(1)} %pad_clamp_fusion), kind=kCustom, calls=%fused_computation.1.clone | custom fusion | bytes 786944 | tf_op jit(solution)/shard_map/jit(_take)/gather | solution.py:93
  12.1 0.0 copy-start.1
  12.1 0.1 select_bitcast_fusion
  12.2 1.1 %copy.37 = bf16[2,2,128,384]{3,1,0,2:T(2,128)(2,1)} copy(bf16[2,2,128,384]{3,2,1,0:T(8,128)(2,1)S(1)} %select_bitcast_fusion) | data formatting | bytes 786432 | tf_op jit(solution)/shard_map/jit(_take)/select_n | solution.py:93
  13.4 6.1 %all-to-all-start.1 = ((bf16[2,2,128,384]{3,1,0,2:T(2,128)(2,1)}), bf16[2,2,128,384]{3,1,0,2:T(2,128)(2,1)S(1)}, u32[]{:S(2)}, u32[]{:S(2)}) async-start(bf16[2,2,128,384]{3,1,0,2:T(2,128)(2,1)} %copy.37), calls=%async_computation.1 | async-start | bytes 786432 | tf_op jit(solution)/shard_map/all_to_all | solution.py:117
  19.5 0.1 copy.71
  19.5 0.1 fusion.50
  19.6 0.1 fusion.52
  19.7 0.0 collective-permute-done
  19.7 2.3 %collective-permute-done.1 = bf16[2,2,192,384]{3,2,1,0:T(8,128)(2,1)} collective-permute-done((bf16[2,2,192,384]{3,2,1,0:T(8,128)(2,1)}, bf16[2,2,192,384]{3,2,1,0:T(8,128)(2,1)}, u32[]{:S(2)}, u32[]{:S(2)}) %collective-permute-start.1) | collective-permute-done | bytes 589856 | tf_op jit(solution)/shard_map/ppermute | solution.py:21
  22.0 1.2 %pad_maximum_fusion = bf16[2,2,576,384]{3,2,1,0:T(8,128)(2,1)S(1)} fusion(bf16[2,2,192,384]{3,2,1,0:T(8,128)(2,1)} %collective-permute-done.1, bf16[2,2,192,384]{3,2,1,0:T(8,128)(2,1)S(1)} %copy-done.2, bf16[2,2,192,384]{3,2,1,0:T(8,128)(2,1)S(1)} %collective-permute-done), kind=kLoop, calls=%fused_computation.7 | loop fusion | flops 5308416 | bytes 3538944 | tf_op jit(solution)/shard_map/concatenate | solution.py:17
  23.3 0.2 slice_bitcast_fusion
  23.5 0.4 fusion.35
  23.9 0.1 slice_bitcast_fusion.3
  24.0 0.5 convolution_convert_fusion
  24.5 0.4 fusion.28
  24.9 0.2 fusion.83
  25.1 0.5 convolution_convert_fusion.1
  25.6 0.4 fusion.30
  26.0 0.2 fusion.84
  26.2 0.5 convolution_convert_fusion.2
  26.7 0.2 fusion.85
  26.9 0.4 fusion.25
  27.3 0.4 fusion.22
  27.7 0.4 fusion.19
  28.1 0.4 fusion.32
  28.5 0.7 fusion.5
  29.2 0.6 copy.35
  29.8 1.5 %gather_fusion = bf16[128,2,2,384]{3,2,1,0:T(2,128)(2,1)S(1)} fusion(bf16[2,2,192,384]{3,1,2,0:T(2,128)(2,1)S(1)} %copy.35, s32[1024]{0:T(1024)S(1)} %pad_clamp_fusion), kind=kCustom, calls=%fused_computation.clone | custom fusion | bytes 786944 | tf_op jit(solution)/shard_map/jit(_take)/gather | solution.py:114
  31.3 1.2 %fusion.38 = bf16[2,2,128,384]{3,1,0,2:T(2,128)(2,1)} fusion(bf16[128,2,2,384]{3,2,1,0:T(2,128)(2,1)S(1)} %gather_fusion, pred[128]{0:T(512)(128)(4,1)S(1)} %get-tuple-element.8), kind=kLoop, calls=%fused_computation.83 | loop fusion | flops 196608 | bytes 786560 | tf_op jit(solution)/shard_map/jit(_take)/select_n | solution.py:114
  32.6 5.9 %all-to-all-start = ((bf16[2,2,128,384]{3,1,0,2:T(2,128)(2,1)}), bf16[2,2,128,384]{3,1,0,2:T(2,128)(2,1)S(1)}, u32[]{:S(2)}, u32[]{:S(2)}) async-start(bf16[2,2,128,384]{3,1,0,2:T(2,128)(2,1)} %fusion.38), calls=%async_computation | async-start | bytes 786432 | tf_op jit(solution)/shard_map/all_to_all | solution.py:116
  38.5 0.1 copy.72
  38.6 0.2 reshape.146
  38.8 0.2 fusion.89
  39.0 0.3 convolution_add_fusion.1
  39.3 0.1 copy.60
  39.5 0.2 fusion.90
  39.7 0.3 convolution_add_fusion
  40.1 0.1 copy.61
  40.2 10.5 %all-to-all-done = bf16[2,2,128,384]{3,1,0,2:T(2,128)(2,1)S(1)} async-done(((bf16[2,2,128,384]{3,1,0,2:T(2,128)(2,1)}), bf16[2,2,128,384]{3,1,0,2:T(2,128)(2,1)S(1)}, u32[]{:S(2)}, u32[]{:S(2)}) %all-to-all-start) | async-done | bytes 393248 | tf_op jit(solution)/shard_map/all_to_all | solution.py:116
  50.7 0.1 copy.73
  50.8 0.2 reshape.143
  50.9 0.2 fusion.87
  51.2 0.2 fusion.88
  51.4 0.3 convolution_add_fusion.3
  51.8 0.1 copy.58
  51.9 0.3 convolution_add_fusion.2
  52.2 0.1 copy.59
  52.4 0.6 multiply_subtract_fusion
  53.0 0.2 fusion.86
  53.3 0.7 fusion.15
  53.9 0.7 fusion.17
  54.6 0.3 fusion.34
  55.0 0.2 fusion.14
  55.2 0.1 copy.41
  55.3 15.5 %all_to_all.48 = bf16[32,2,8,384]{3,2,1,0:T(8,128)(2,1)S(1)} all-to-all(bf16[32,2,8,384]{3,2,1,0:T(8,128)(2,1)S(1)} %copy.41), channel_id=1, replica_groups=mesh['slab'=2,'energy'=16] {'energy'}, dimensions={0} | all-to-all | bytes 786432 | tf_op jit(solution)/shard_map/all_to_all | solution.py:120
  70.8 0.3 copy.42
  71.1 0.3 broadcast_in_dim.17
  71.4 5.9 %scatter_fusion = bf16[2,2,192,384]{3,1,2,0:T(2,128)(2,1)S(1)} fusion(bf16[2,2,192,384]{3,1,2,0:T(2,128)(2,1)S(1)} %broadcast_in_dim.17, s32[128]{0:T(128)S(1)} %get-tuple-element.9, bf16[128,2,2,384]{3,2,1,0:T(2,128)(2,1)S(1)} %bitcast.190), kind=kCustom, calls=%fused_computation.2 | custom fusion | bytes 1180160 | tf_op jit(solution)/shard_map/scatter | solution.py:122
  77.4 0.9 %copy.43 = bf16[2,2,192,384]{3,2,1,0:T(8,128)(2,1)} copy(bf16[2,2,192,384]{3,1,2,0:T(2,128)(2,1)S(1)} %scatter_fusion) | data formatting | bytes 1179648 | tf_op jit(solution)/shard_map/scatter | solution.py:122
  (9 shorter events, 0.0 us)
Async XLA Ops:
  0.0 10.2 %copy-start = (bf16[2,2,192,384]{3,2,1,0:T(8,128)(2,1)S(1)}, bf16[2,2,192,384]{3,2,1,0:T(8,128)(2,1)}, u32[]{:S(2)}) copy-start(bf16[2,2,192,384]{3,2,1,0:T(8,128)(2,1)} %param.8) | copy-start | bytes 1769476
  0.0 19.7 %collective-permute-start = (bf16[2,2,192,384]{3,2,1,0:T(8,128)(2,1)}, bf16[2,2,192,384]{3,2,1,0:T(8,128)(2,1)S(1)}, u32[]{:S(2)}, u32[]{:S(2)}) collective-permute-start(bf16[2,2,192,384]{3,2,1,0:T(8,128)(2,1)} %param.7), channel_id=1, source_target_pairs={{0,16},{1,17},{2,18},{3,19},{4,20},{5,21},{6,22},{7,23},{8,24},{9,... | collective-permute-start | bytes 1769480 | tf_op jit(solution)/shard_map/ppermute | solution.py:19
  5.0 17.0 %collective-permute-start.1 = (bf16[2,2,192,384]{3,2,1,0:T(8,128)(2,1)}, bf16[2,2,192,384]{3,2,1,0:T(8,128)(2,1)}, u32[]{:S(2)}, u32[]{:S(2)}) collective-permute-start(bf16[2,2,192,384]{3,2,1,0:T(8,128)(2,1)} %param.7), channel_id=1, source_target_pairs={{16,0},{17,1},{18,2},{19,3},{20,4},{21,5},{22,6},{23,7},{24,8},{25... | collective-permute-start | bytes 1769480 | tf_op jit(solution)/shard_map/ppermute | solution.py:21
  12.1 7.4 %copy-start.1 = (bf16[2,3,192,384]{3,2,1,0:T(8,128)(2,1)S(1)}, bf16[2,3,192,384]{3,2,1,0:T(8,128)(2,1)}, u32[]{:S(2)}) copy-start(bf16[2,3,192,384]{3,2,1,0:T(8,128)(2,1)} %param.6) | copy-start | bytes 2654212
  13.4 8.7 %copy-start.2 = (bf16[2,2,192,384]{3,2,1,0:T(8,128)(2,1)S(1)}, bf16[2,2,192,384]{3,2,1,0:T(8,128)(2,1)}, u32[]{:S(2)}) copy-start(bf16[2,2,192,384]{3,2,1,0:T(8,128)(2,1)} %param.7) | copy-start | bytes 1769476
  13.4 19.2 %all-to-all-start.1 = ((bf16[2,2,128,384]{3,1,0,2:T(2,128)(2,1)}), bf16[2,2,128,384]{3,1,0,2:T(2,128)(2,1)S(1)}, u32[]{:S(2)}, u32[]{:S(2)}) async-start(bf16[2,2,128,384]{3,1,0,2:T(2,128)(2,1)} %copy.37), calls=%async_computation.1 | async-start | bytes 786432 | tf_op jit(solution)/shard_map/all_to_all | solution.py:117
  32.6 18.1 %all-to-all-start = ((bf16[2,2,128,384]{3,1,0,2:T(2,128)(2,1)}), bf16[2,2,128,384]{3,1,0,2:T(2,128)(2,1)S(1)}, u32[]{:S(2)}, u32[]{:S(2)}) async-start(bf16[2,2,128,384]{3,1,0,2:T(2,128)(2,1)} %fusion.38), calls=%async_computation | async-start | bytes 786432 | tf_op jit(solution)/shard_map/all_to_all | solution.py:116
where the time goes:
time: 78.7 us; the launch traced here: 78.3 us
  starting transfers between devices  18.3 us (23%)
  blocking collectives  15.5 us (20%)
  local copies, waits for them, and re-layouts  14.1 us (18%)
  waiting for transfers between devices  12.8 us (16%)
  other arithmetic  9.58 us (12%)
  matrix products  7.6 us (10%)
    all_to_all x1, blocking collectives, local(): lax.all_to_all(sigma, 'energy', split_axis=0, concat_axis=2, tiled=True)  15.5 us
    all_to_all x1, waiting for transfers between devices, local(): lax.all_to_all(green_send, 'energy', split_axis=2, concat_axis=0, tiled=T...  10.5 us
    scatter x2, local copies, waits for them, and re-layouts, local(): result = result.at[:, :, live_order, :].set(returned_rows)  6.8 us
    all_to_all x1, starting transfers between devices, local(): lax.all_to_all(screen_send, 'energy', split_axis=2, concat_axis=0, tiled=...  6.07 us
    all_to_all x1, starting transfers between devices, local(): lax.all_to_all(green_send, 'energy', split_axis=2, concat_axis=0, tiled=T...  5.95 us
    ppermute x1, starting transfers between devices, with_halo(): lax.ppermute(tail, axis, [(i, (i + 1) % count) for i in range(ends)])  5 us
    sort x1, other arithmetic, local(): live_order = jnp.argsort(1 - pattern, stable=True)[:live_count]  3.17 us
    ppermute x1, waiting for transfers between devices, with_halo(): lax.ppermute(head, axis, [((i + 1) % count, i) for i in range(ends)])  2.28 us
  transfers between devices with their start and end apart: 4, of which 2 were waited for; matrix products, arithmetic and copies ran while one was open for 25% of the time, Pallas kernels for 0%

commit v1 on v0

v1 whole, which is shorter than its diff:
```python
import functools
import math

import jax
import jax.numpy as jnp
import numpy as np
from jax import lax
from jax.experimental import pallas as pl
from jax.experimental.pallas import tpu as pltpu
from jax.sharding import PartitionSpec as P

MESH = pl.DeviceIdType.MESH
F32 = jnp.float32
BF16 = jnp.bfloat16


def dot(a, b):
    return jnp.dot(a, b, preferred_element_type=F32)


def dot_nt(a, b):
    return lax.dot_general(a, b, (((1,), (1,)), ((), ())), preferred_element_type=F32)


def times_i(x):
    half = x.shape[-1] // 2
    lane = lax.broadcasted_iota(jnp.int32, x.shape, 1)
    turned = pltpu.roll(x, half, 1)
    return jnp.where(lane < half, -turned, turned)


def complex_times(x, y):
    half = x.shape[-1] // 2
    first = lax.broadcasted_iota(jnp.int32, x.shape, 1) < half
    turned = pltpu.roll(y, half, 1)
    return x * jnp.where(first, y, turned) + times_i(x) * jnp.where(first, turned, y)


def kernel(
    retarded, injection, screened, pattern, tables, want_slot, want_col, want_row,
    result,
    ret_v, inj_v, scr_v, tab_v, halo, row_wide, row_live, total, screen_hat, out_v,
    s_send, s_recv, g_send, g_recv, c_send, c_recv,
    load_sem, halo_out, halo_in, s_out, s_in, g_out, g_in, c_out, c_in, store_sem,
):
    owners = lax.axis_size("energy")
    slabs = lax.axis_size("slab")
    me = lax.axis_index("energy")
    slab = lax.axis_index("slab")
    has_left = slab > 0
    has_right = slab < slabs - 1
    energies, _, block, width = ret_v.shape
    chunk = s_send.shape[2]
    per_energy = chunk // energies
    flat = owners * chunk
    count = owners * energies

    loads = [
        pltpu.make_async_copy(source, target, load_sem.at[at])
        for at, (source, target) in enumerate(
            [(screened, scr_v), (retarded, ret_v), (injection, inj_v), (tables, tab_v)]
        )
    ]
    for load in loads:
        load.start()

    barrier = pltpu.get_barrier_semaphore()

    def greet(step, carry):
        peer = lax.rem(me + step, owners)
        pl.semaphore_signal(barrier, inc=1, device_id={"energy": peer}, device_id_type=MESH)
        return carry

    lax.fori_loop(1, owners, greet, 0)

    @pl.when(has_left)
    def _():
        pl.semaphore_signal(barrier, inc=1, device_id={"slab": slab - 1}, device_id_type=MESH)

    @pl.when(has_right)
    def _():
        pl.semaphore_signal(barrier, inc=1, device_id={"slab": slab + 1}, device_id_type=MESH)

    pl.semaphore_wait(
        barrier, owners - 1 + has_left.astype(jnp.int32) + has_right.astype(jnp.int32)
    )

    def halo_copy(side, kind):
        return pltpu.make_async_remote_copy(
            src_ref=injection.at[:, kind],
            dst_ref=halo.at[side, kind],
            send_sem=halo_out.at[side, kind],
            recv_sem=halo_in.at[side, kind],
            device_id={"slab": slab + 1 - 2 * side},
            device_id_type=MESH,
        )

    for kind in range(2):
        @pl.when(has_right)
        def _():
            halo_copy(0, kind).start()

        @pl.when(has_left)
        def _():
            halo_copy(1, kind).start()

    def spread(source, target, out_sem, in_sem):
        def send(step, carry):
            peer = lax.rem(me + step, owners)
            pltpu.make_async_remote_copy(
                src_ref=source.at[peer],
                dst_ref=target.at[me],
                send_sem=out_sem,
                recv_sem=in_sem,
                device_id={"energy": peer},
                device_id_type=MESH,
            ).start()
            return carry

        lax.fori_loop(1, owners, send, 0)
        target[me] = source[me]

    def wait_all(buffer, sem):
        rest = buffer.at[pl.ds(0, owners - 1)]
        pltpu.make_async_copy(rest, rest, sem).wait()

    pattern_row = pattern[...].astype(F32)
    down = lax.broadcasted_iota(jnp.int32, (block, block), 0)
    across = lax.broadcasted_iota(jnp.int32, (block, block), 1)
    pattern_col = jnp.sum(jnp.where(down == across, pattern_row, 0.0), 1, keepdims=True)
    rank_col = jnp.sum(jnp.where(across < down, pattern_row, 0.0), 1, keepdims=True)
    rank_row = jnp.sum(jnp.where(down < across, pattern_col, 0.0), 0, keepdims=True)
    key_col = jnp.where(pattern_col > 0.5, rank_col, -1.0)
    key_row = jnp.where(pattern_row > 0.5, rank_row, -1.0)

    def one_hot(left, right):
        return jnp.where(left == right, 1.0, 0.0).astype(BF16)

    loads[0].wait()
    picks = [one_hot(want_col[e], key_row) for e in range(energies)]
    for kind in range(2):
        picked = sum(dot(picks[e], scr_v[e, kind]) for e in range(energies))
        s_send[:, kind] = picked.astype(BF16).reshape(owners, chunk, width)
    spread(s_send, s_recv, s_out, s_in)

    pick_rows = one_hot(want_slot[...], key_row)

    def widen(x):
        return times_i(x.astype(F32)).astype(BF16)

    def prepare(offset):
        for e in range(energies):
            rows = ret_v[e, offset]
            row_wide[offset, e, :block] = rows
            row_wide[offset, e, block:] = widen(rows)
            row_live[offset, e] = dot(pick_rows, rows).astype(BF16)

    def term(offset, e, inject):
        expanded = jnp.concatenate([inject, widen(inject)], 0)
        left = dot(row_live[offset, e], expanded).astype(BF16)
        return dot_nt(left, row_wide[offset, e])

    loads[1].wait()
    loads[2].wait()
    prepare(1)

    @pl.when(has_left)
    def _():
        prepare(0)

    @pl.when(has_right)
    def _():
        prepare(2)

    for kind in range(2):
        for e in range(energies):
            total[kind, e] = term(1, e, inj_v[e, kind])

    def green(kind):
        @pl.when(has_left)
        def _():
            halo_copy(0, kind).wait_recv()
            for e in range(energies):
                total[kind, e] += term(0, e, halo[0, kind, e])

        @pl.when(has_right)
        def _():
            halo_copy(1, kind).wait_recv()
            for e in range(energies):
                total[kind, e] += term(2, e, halo[1, kind, e])

        parts = [total[kind, e].reshape(owners, per_energy, width) for e in range(energies)]
        g_send[kind] = jnp.concatenate(parts, 1).astype(BF16)
        spread(g_send.at[kind], g_recv.at[kind], g_out.at[kind], g_in.at[kind])

    def forward(values):
        with_cos = dot(tab_v[0], values) + dot(tab_v[2], values)
        with_sin = dot(tab_v[1], values) + dot(tab_v[3], values)
        return with_cos - times_i(with_sin)

    factor = 1.0 / (count * math.sqrt(count))

    def convolve(kind):
        wait_all(g_recv.at[kind], g_in.at[kind])
        green_hat = forward(g_recv[kind].reshape(flat, width))
        product = complex_times(green_hat, screen_hat[kind])
        high = product.astype(BF16)
        low = (product - high.astype(F32)).astype(BF16)
        with_cos = dot(tab_v[0], high) + dot(tab_v[2], high) + dot(tab_v[0], low)
        with_sin = dot(tab_v[1], high) + dot(tab_v[3], high) + dot(tab_v[1], low)
        sigma = (times_i(with_cos) - with_sin) * factor
        c_send[kind] = sigma.astype(BF16).reshape(owners, chunk, width)
        spread(c_send.at[kind], c_recv.at[kind], c_out.at[kind], c_in.at[kind])

    green(0)
    loads[3].wait()
    wait_all(s_recv, s_in)
    for kind in range(2):
        screen_hat[kind] = forward(s_recv[:, kind].reshape(flat, width))
    green(1)
    convolve(0)
    convolve(1)

    places = [one_hot(key_col, want_row[e]) for e in range(energies)]
    stores = []
    for kind in range(2):
        wait_all(c_recv.at[kind], c_in.at[kind])
        back = c_recv[kind].reshape(flat, width)
        for e in range(energies):
            out_v[kind, e] = dot(places[e], back).astype(BF16)
        store = pltpu.make_async_copy(out_v.at[kind], result.at[:, kind], store_sem.at[kind])
        store.start()
        stores.append(store)

    for kind in range(2):
        @pl.when(has_right)
        def _():
            halo_copy(0, kind).wait_send()

        @pl.when(has_left)
        def _():
            halo_copy(1, kind).wait_send()

    wait_all(s_send, s_out)
    for kind in range(2):
        wait_all(g_send.at[kind], g_out.at[kind])
        wait_all(c_send.at[kind], c_out.at[kind])
        stores[kind].wait()


def layout(owners, energies, live):
    share = -(-live // owners)
    padded = -(-share // 8) * 8
    while energies * padded % 16:
        padded += 8
    slot = np.arange(owners * padded)
    wanted = slot // padded * share + slot % padded
    wanted = np.where((slot % padded < share) & (wanted < live), wanted, -2)
    by_energy = np.full((energies, owners, energies, padded), -2)
    for e in range(energies):
        by_energy[e, :, e] = wanted.reshape(owners, padded)
    by_energy = by_energy.reshape(energies, -1)
    count = owners * energies
    index = np.arange(count)
    angle = 2.0 * np.pi / count * (index[:, None] * index[None, :] % count)
    tables = np.stack([np.cos(angle), np.sin(angle)]).astype(np.float32)
    high = tables.astype(jnp.bfloat16)
    low = (tables - high.astype(np.float32)).astype(jnp.bfloat16)
    small = np.concatenate([high, low]).astype(np.float32)
    eye = np.eye(padded, dtype=np.float32)
    wide = np.stack([np.kron(table, eye) for table in small]).astype(jnp.bfloat16)
    return padded, wanted.astype(np.float32), by_energy.astype(np.float32), wide


def local(retarded, injection, screened, pattern):
    energies, _, block, width = retarded.shape
    owners = lax.axis_size("energy")
    live = block * 2 // 3
    padded, wanted, by_energy, tables = layout(owners, energies, live)
    chunk = energies * padded
    flat = owners * chunk
    slots = owners * padded
    anywhere = pl.BlockSpec(memory_space=pl.ANY)
    vmem = pl.BlockSpec(memory_space=pltpu.VMEM)
    dma = pltpu.SemaphoreType.DMA
    blocks = (2, owners, chunk, width)
    return pl.pallas_call(
        kernel,
        out_shape=jax.ShapeDtypeStruct(screened.shape, BF16),
        in_specs=[anywhere] * 3 + [vmem, anywhere] + [vmem] * 3,
        out_specs=anywhere,
        scratch_shapes=[
            pltpu.VMEM(retarded.shape, BF16),
            pltpu.VMEM(injection.shape, BF16),
            pltpu.VMEM(screened.shape, BF16),
            pltpu.VMEM(tables.shape, BF16),
            pltpu.VMEM((2, 2, energies, block, width), BF16),
            pltpu.VMEM((3, energies, 2 * block, width), BF16),
            pltpu.VMEM((3, energies, slots, width), BF16),
            pltpu.VMEM((2, energies, slots, width), F32),
            pltpu.VMEM((2, flat, width), F32),
            pltpu.VMEM((2, energies, block, width), BF16),
            pltpu.VMEM((owners, 2, chunk, width), BF16),
            pltpu.VMEM((owners, 2, chunk, width), BF16),
            pltpu.VMEM(blocks, BF16),
            pltpu.VMEM(blocks, BF16),
            pltpu.VMEM(blocks, BF16),
            pltpu.VMEM(blocks, BF16),
            dma((4,)),
            dma((2, 2)),
            dma((2, 2)),
            dma,
            dma,
            dma((2,)),
            dma((2,)),
            dma((2,)),
            dma((2,)),
            dma((2,)),
        ],
        compiler_params=pltpu.CompilerParams(
            collective_id=0, has_side_effects=True, vmem_limit_bytes=56 * 1024 * 1024
        ),
    )(
        retarded,
        injection,
        screened,
        pattern.reshape(1, -1),
        jnp.asarray(tables),
        jnp.asarray(wanted.reshape(-1, 1)),
        jnp.asarray(by_energy.reshape(energies, -1, 1)),
        jnp.asarray(by_energy.reshape(energies, 1, -1)),
    )


def solution(mesh):
    placed = (
        P("energy", None, "slab", None),
        P("energy", None, "slab", None),
        P("energy", None, "slab", None),
        P("slab"),
    )
    return jax.shard_map(
        local,
        mesh=mesh,
        in_specs=placed,
        out_specs=P("energy", None, "slab", None),
        check_vma=False,
    )
```

time: 78.7 us -> 39.2 us (0.50)
  Pallas kernels: 0 us -> 37.1 us
  starting transfers between devices: 18.3 us -> 0 us
  blocking collectives: 15.5 us -> 0 us
  waiting for transfers between devices: 12.8 us -> 0 us
  local copies, waits for them, and re-layouts: 14.1 us -> 1.94 us
  other arithmetic: 9.58 us -> 0 us
  matrix products: 7.6 us -> 0 us
    pallas_call x0 -> x1, Pallas kernels: none -> 37.1 us  [local(): pl.pallas_call(kernel, out_shape=jax.ShapeDtypeStruct(screened.shape, BF1...]
    all_to_all x1 -> x0, blocking collectives: 15.5 us -> none  [local(): lax.all_to_all(sigma, 'energy', split_axis=0, concat_axis=2, tiled=True)]
    all_to_all x2 -> x0, starting transfers between devices: 12 us -> none  [the longest x1 6.07 us: local(): lax.all_to_all(screen_send, 'energy', split_axis=2, concat_axis=0, tiled=...]
    all_to_all x2 -> x0, waiting for transfers between devices: 10.5 us -> none  [the longest x1 10.5 us: local(): lax.all_to_all(green_send, 'energy', split_axis=2, concat_axis=0, tiled=T...]
    dot_general x19 -> x0, matrix products: 7.6 us -> none  [the longest x3 1.58 us: local(): jnp.einsum('enac,elncd->elnad', row_block, expanded, preferred_element_ty...]
    scatter x2 -> x0, local copies, waits for them, and re-layouts: 6.8 us -> none  [local(): result = result.at[:, :, live_order, :].set(returned_rows)]
    ppermute x2 -> x0, starting transfers between devices: 6.29 us -> none  [the longest x1 5 us: with_halo(): lax.ppermute(tail, axis, [(i, (i + 1) % count) for i in range(ends)])]
    gather x2 -> x0, local copies, waits for them, and re-layouts: 3.37 us -> none  [the longest x1 1.88 us: local(): screen_send = jnp.take(screened, live_order, axis=2)]
  transfers between devices with their start and end apart: 4 -> 0, of which waited for: 2 -> 0; matrix products, arithmetic and copies ran while one was open for 25% -> 0% of each run, Pallas kernels for 0% -> 0%
where the time goes in v1:
time: 39.2 us; the launch traced here: 39.1 us
  Pallas kernels  37.1 us (95%)
  local copies, waits for them, and re-layouts  1.94 us (5%)
    pallas_call x1, Pallas kernels, local(): pl.pallas_call(kernel, out_shape=jax.ShapeDtypeStruct(screened.shape, BF1...  37.1 us
    unnamed x1, local copies, waits for them, and re-layouts  1.94 us

profile of v1, /device:TPU:0, one launch (start us, length us, event | category | flops | bytes accessed | tf_op | source)
XLA Modules:
  0.0 39.1 jit_solution(1709447489307061922)
XLA Ops:
  0.0 37.1 %shard_map.82 = bf16[2,2,192,384]{3,2,1,0:T(8,128)(2,1)} custom-call(bf16[2,3,192,384]{3,2,1,0:T(8,128)(2,1)} %retarded.1, bf16[2,2,192,384]{3,2,1,0:T(8,128)(2,1)} %injection.1, bf16[2,2,192,384]{3,2,1,0:T(8,128)(2,1)} %screened.1, s32[1,192]{1,0:T(1,128)} %bitcast.1, bf16[4,256,256]{2,1,0:T(8,128)(2,1)} %constant.8.clone.tables, ...), custom_call_target="tpu_custom_call" | custom-call | tf_op jit(solution)/shard_map/pallas_call | solution.py:287
  37.1 1.9 %copy.10 = bf16[2,2,192,384]{3,2,1,0:T(8,128)(2,1)} copy(bf16[2,2,192,384]{3,2,1,0:T(8,128)(2,1)} %shard_map.82) | data formatting | bytes 1179648

commit v2 on v1

--- a/solution.py
+++ b/solution.py
@@ -1,4 +1,3 @@
-import functools
 import math
 
 import jax
@@ -38,10 +37,11 @@
 
 def kernel(
     retarded, injection, screened, pattern, tables, want_slot, want_col, want_row,
-    result,
-    ret_v, inj_v, scr_v, tab_v, halo, row_wide, row_live, total, screen_hat, out_v,
-    s_send, s_recv, g_send, g_recv, c_send, c_recv,
-    load_sem, halo_out, halo_in, s_out, s_in, g_out, g_in, c_out, c_in, store_sem,
+    back, places,
+    ret_v, inj_v, scr_v, pat_v, tab_v, slot_v, col_v, row_v,
+    halo, row_wide, row_live, total, screen_hat,
+    places_v, s_send, s_recv, g_send, g_recv, c_send,
+    load_sem, halo_out, halo_in, s_out, s_in, g_out, g_in, c_out, c_in, own_sem, store_sem,
 ):
     owners = lax.axis_size("energy")
     slabs = lax.axis_size("slab")
@@ -58,7 +58,16 @@
     loads = [
         pltpu.make_async_copy(source, target, load_sem.at[at])
         for at, (source, target) in enumerate(
-            [(screened, scr_v), (retarded, ret_v), (injection, inj_v), (tables, tab_v)]
+            [
+                (pattern, pat_v),
+                (want_col, col_v),
+                (screened, scr_v),
+                (want_slot, slot_v),
+                (retarded, ret_v),
+                (injection, inj_v),
+                (tables, tab_v),
+                (want_row, row_v),
+            ]
         )
     ]
     for load in loads:
@@ -80,6 +89,51 @@
     @pl.when(has_right)
     def _():
         pl.semaphore_signal(barrier, inc=1, device_id={"slab": slab + 1}, device_id_type=MESH)
+
+    def spread(source, target, out_sem, in_sem):
+        half = owners // 2
+        while half:
+            group = me // half
+            first = (group + 1 - 2 * lax.rem(group, 2)) * half
+
+            def send(step, carry, half=half, first=first):
+                peer = first + lax.rem(me + step, half)
+                pltpu.make_async_remote_copy(
+                    src_ref=source.at[peer],
+                    dst_ref=target.at[me],
+                    send_sem=out_sem,
+                    recv_sem=in_sem,
+                    device_id={"energy": peer},
+                    device_id_type=MESH,
+                ).start()
+                return carry
+
+            lax.fori_loop(0, half, send, 0)
+            half //= 2
+
+    def wait_all(buffer, sem):
+        rest = buffer.at[pl.ds(0, owners - 1)]
+        pltpu.make_async_copy(rest, rest, sem).wait()
+
+    loads[0].wait()
+    pattern_row = pat_v[...].astype(F32)
+    down = lax.broadcasted_iota(jnp.int32, (block, block), 0)
+    across = lax.broadcasted_iota(jnp.int32, (block, block), 1)
+    pattern_col = jnp.sum(jnp.where(down == across, pattern_row, 0.0), 1, keepdims=True)
+    rank_col = jnp.sum(jnp.where(across < down, pattern_row, 0.0), 1, keepdims=True)
+    rank_row = jnp.sum(jnp.where(down < across, pattern_col, 0.0), 0, keepdims=True)
+    key_col = jnp.where(pattern_col > 0.5, rank_col, -1.0)
+    key_row = jnp.where(pattern_row > 0.5, rank_row, -1.0)
+
+    def one_hot(left, right):
+        return jnp.where(left == right, 1.0, 0.0).astype(BF16)
+
+    loads[1].wait()
+    picks = [one_hot(col_v[e], key_row) for e in range(energies)]
+    loads[2].wait()
+    for kind in range(2):
+        picked = sum(dot(picks[e], scr_v[e, kind]) for e in range(energies))
+        s_send[:, kind] = picked.astype(BF16).reshape(owners, chunk, width)
 
     pl.semaphore_wait(
         barrier, owners - 1 + has_left.astype(jnp.int32) + has_right.astype(jnp.int32)
@@ -104,46 +158,11 @@
         def _():
             halo_copy(1, kind).start()
 
-    def spread(source, target, out_sem, in_sem):
-        def send(step, carry):
-            peer = lax.rem(me + step, owners)
-            pltpu.make_async_remote_copy(
-                src_ref=source.at[peer],
-                dst_ref=target.at[me],
-                send_sem=out_sem,
-                recv_sem=in_sem,
-                device_id={"energy": peer},
-                device_id_type=MESH,
-            ).start()
-            return carry
-
-        lax.fori_loop(1, owners, send, 0)
-        target[me] = source[me]
-
-    def wait_all(buffer, sem):
-        rest = buffer.at[pl.ds(0, owners - 1)]
-        pltpu.make_async_copy(rest, rest, sem).wait()
-
-    pattern_row = pattern[...].astype(F32)
-    down = lax.broadcasted_iota(jnp.int32, (block, block), 0)
-    across = lax.broadcasted_iota(jnp.int32, (block, block), 1)
-    pattern_col = jnp.sum(jnp.where(down == across, pattern_row, 0.0), 1, keepdims=True)
-    rank_col = jnp.sum(jnp.where(across < down, pattern_row, 0.0), 1, keepdims=True)
-    rank_row = jnp.sum(jnp.where(down < across, pattern_col, 0.0), 0, keepdims=True)
-    key_col = jnp.where(pattern_col > 0.5, rank_col, -1.0)
-    key_row = jnp.where(pattern_row > 0.5, rank_row, -1.0)
-
-    def one_hot(left, right):
-        return jnp.where(left == right, 1.0, 0.0).astype(BF16)
-
-    loads[0].wait()
-    picks = [one_hot(want_col[e], key_row) for e in range(energies)]
-    for kind in range(2):
-        picked = sum(dot(picks[e], scr_v[e, kind]) for e in range(energies))
-        s_send[:, kind] = picked.astype(BF16).reshape(owners, chunk, width)
     spread(s_send, s_recv, s_out, s_in)
-
-    pick_rows = one_hot(want_slot[...], key_row)
+    s_recv[me] = s_send[me]
+
+    loads[3].wait()
+    pick_rows = one_hot(slot_v[...], key_row)
 
     def widen(x):
         return times_i(x.astype(F32)).astype(BF16)
@@ -160,8 +179,8 @@
         left = dot(row_live[offset, e], expanded).astype(BF16)
         return dot_nt(left, row_wide[offset, e])
 
-    loads[1].wait()
-    loads[2].wait()
+    loads[4].wait()
+    loads[5].wait()
     prepare(1)
 
     @pl.when(has_left)
@@ -192,11 +211,14 @@
         parts = [total[kind, e].reshape(owners, per_energy, width) for e in range(energies)]
         g_send[kind] = jnp.concatenate(parts, 1).astype(BF16)
         spread(g_send.at[kind], g_recv.at[kind], g_out.at[kind], g_in.at[kind])
+        g_recv[kind, me] = g_send[kind, me]
+
+    def transform(pieces):
+        return dot(tab_v[:, : flat * len(pieces)], jnp.concatenate(pieces, 0))
 
     def forward(values):
-        with_cos = dot(tab_v[0], values) + dot(tab_v[2], values)
-        with_sin = dot(tab_v[1], values) + dot(tab_v[3], values)
-        return with_cos - times_i(with_sin)
+        turned = widen(values)
+        return transform([values, turned, values, turned])
 
     factor = 1.0 / (count * math.sqrt(count))
 
@@ -204,33 +226,30 @@
         wait_all(g_recv.at[kind], g_in.at[kind])
         green_hat = forward(g_recv[kind].reshape(flat, width))
         product = complex_times(green_hat, screen_hat[kind])
-        high = product.astype(BF16)
+        turned = times_i(product)
+        high, turned_high = product.astype(BF16), turned.astype(BF16)
         low = (product - high.astype(F32)).astype(BF16)
-        with_cos = dot(tab_v[0], high) + dot(tab_v[2], high) + dot(tab_v[0], low)
-        with_sin = dot(tab_v[1], high) + dot(tab_v[3], high) + dot(tab_v[1], low)
-        sigma = (times_i(with_cos) - with_sin) * factor
-        c_send[kind] = sigma.astype(BF16).reshape(owners, chunk, width)
-        spread(c_send.at[kind], c_recv.at[kind], c_out.at[kind], c_in.at[kind])
+        turned_low = (turned - turned_high.astype(F32)).astype(BF16)
+        sigma = transform([turned_high, high, turned_high, high, turned_low, low])
+        c_send[kind] = (sigma * factor).astype(BF16).reshape(owners, chunk, width)
+        spread(c_send.at[kind], back.at[kind], c_out.at[kind], c_in.at[kind])
+        own = pltpu.make_async_copy(c_send.at[kind, me], back.at[kind, me], own_sem.at[kind])
+        own.start()
+        return own
 
     green(0)
-    loads[3].wait()
+    loads[6].wait()
     wait_all(s_recv, s_in)
     for kind in range(2):
         screen_hat[kind] = forward(s_recv[:, kind].reshape(flat, width))
     green(1)
-    convolve(0)
-    convolve(1)
-
-    places = [one_hot(key_col, want_row[e]) for e in range(energies)]
-    stores = []
-    for kind in range(2):
-        wait_all(c_recv.at[kind], c_in.at[kind])
-        back = c_recv[kind].reshape(flat, width)
-        for e in range(energies):
-            out_v[kind, e] = dot(places[e], back).astype(BF16)
-        store = pltpu.make_async_copy(out_v.at[kind], result.at[:, kind], store_sem.at[kind])
-        store.start()
-        stores.append(store)
+    owns = [convolve(0), convolve(1)]
+
+    loads[7].wait()
+    for e in range(energies):
+        places_v[e] = one_hot(key_col, row_v[e])
+    store = pltpu.make_async_copy(places_v, places, store_sem)
+    store.start()
 
     for kind in range(2):
         @pl.when(has_right)
@@ -245,7 +264,17 @@
     for kind in range(2):
         wait_all(g_send.at[kind], g_out.at[kind])
         wait_all(c_send.at[kind], c_out.at[kind])
-        stores[kind].wait()
+        wait_all(back.at[kind], c_in.at[kind])
+        owns[kind].wait()
+    store.wait()
+
+
+def expand(back, places, result):
+    energies, kinds = result.shape[:2]
+    for kind in range(kinds):
+        rows = back[kind].reshape(-1, back.shape[-1])
+        for e in range(energies):
+            result[e, kind] = dot(places[e], rows).astype(BF16)
 
 
 def layout(owners, energies, live):
@@ -268,7 +297,9 @@
     low = (tables - high.astype(np.float32)).astype(jnp.bfloat16)
     small = np.concatenate([high, low]).astype(np.float32)
     eye = np.eye(padded, dtype=np.float32)
-    wide = np.stack([np.kron(table, eye) for table in small]).astype(jnp.bfloat16)
+    cos_high, sin_high, cos_low, sin_low = [np.kron(table, eye) for table in small]
+    wide = [cos_high, -sin_high, cos_low, -sin_low, cos_high, -sin_high]
+    wide = np.concatenate(wide, 1).astype(jnp.bfloat16)
     return padded, wanted.astype(np.float32), by_energy.astype(np.float32), wide
 
 
@@ -284,29 +315,35 @@
     vmem = pl.BlockSpec(memory_space=pltpu.VMEM)
     dma = pltpu.SemaphoreType.DMA
     blocks = (2, owners, chunk, width)
-    return pl.pallas_call(
+    back, places = pl.pallas_call(
         kernel,
-        out_shape=jax.ShapeDtypeStruct(screened.shape, BF16),
-        in_specs=[anywhere] * 3 + [vmem, anywhere] + [vmem] * 3,
-        out_specs=anywhere,
+        out_shape=(
+            jax.ShapeDtypeStruct(blocks, BF16),
+            jax.ShapeDtypeStruct((energies, block, flat), BF16),
+        ),
+        in_specs=[anywhere] * 8,
+        out_specs=(anywhere, anywhere),
         scratch_shapes=[
             pltpu.VMEM(retarded.shape, BF16),
             pltpu.VMEM(injection.shape, BF16),
             pltpu.VMEM(screened.shape, BF16),
+            pltpu.VMEM((1, block), pattern.dtype),
             pltpu.VMEM(tables.shape, BF16),
+            pltpu.VMEM((slots, 1), F32),
+            pltpu.VMEM((energies, flat, 1), F32),
+            pltpu.VMEM((energies, 1, flat), F32),
             pltpu.VMEM((2, 2, energies, block, width), BF16),
             pltpu.VMEM((3, energies, 2 * block, width), BF16),
             pltpu.VMEM((3, energies, slots, width), BF16),
             pltpu.VMEM((2, energies, slots, width), F32),
             pltpu.VMEM((2, flat, width), F32),
-            pltpu.VMEM((2, energies, block, width), BF16),
+            pltpu.VMEM((energies, block, flat), BF16),
             pltpu.VMEM((owners, 2, chunk, width), BF16),
             pltpu.VMEM((owners, 2, chunk, width), BF16),
             pltpu.VMEM(blocks, BF16),
             pltpu.VMEM(blocks, BF16),
             pltpu.VMEM(blocks, BF16),
-            pltpu.VMEM(blocks, BF16),
-            dma((4,)),
+            dma((8,)),
             dma((2, 2)),
             dma((2, 2)),
             dma,
@@ -316,6 +353,7 @@
             dma((2,)),
             dma((2,)),
             dma((2,)),
+            dma,
         ],
         compiler_params=pltpu.CompilerParams(
             collective_id=0, has_side_effects=True, vmem_limit_bytes=56 * 1024 * 1024
@@ -330,6 +368,13 @@
         jnp.asarray(by_energy.reshape(energies, -1, 1)),
         jnp.asarray(by_energy.reshape(energies, 1, -1)),
     )
+    return pl.pallas_call(
+        expand,
+        out_shape=jax.ShapeDtypeStruct(screened.shape, BF16),
+        in_specs=[vmem, vmem],
+        out_specs=vmem,
+        compiler_params=pltpu.CompilerParams(vmem_limit_bytes=32 * 1024 * 1024),
+    )(back, places)
 
 
 def solution(mesh):

time: 39.2 us -> 41.6 us (1.061)
  Pallas kernels: 37.1 us -> 39.5 us
    pallas_call x1 -> x2, Pallas kernels: 37.1 us -> 39.5 us  [the longest x1 38.3 us: local(): pl.pallas_call(kernel, out_shape=(jax.ShapeDtypeStruct(blocks, BF16), jax...]
    unnamed x1 -> x4, local copies, waits for them, and re-layouts: 1.94 us -> 1.92 us
where the time goes in v2:
time: 41.6 us; the launch traced here: 41.4 us
  Pallas kernels  39.5 us (95%)
  local copies, waits for them, and re-layouts  1.92 us (5%)
    pallas_call x1, Pallas kernels, local(): pl.pallas_call(kernel, out_shape=(jax.ShapeDtypeStruct(blocks, BF16), jax...  38.3 us
    unnamed x4, local copies, waits for them, and re-layouts  1.92 us
    pallas_call x1, Pallas kernels, local(): pl.pallas_call(expand, out_shape=jax.ShapeDtypeStruct(screened.shape, BF1...  1.17 us

profile of v2, /device:TPU:0, one launch (start us, length us, event | category | flops | bytes accessed | tf_op | source)
XLA Modules:
  0.0 41.4 jit_solution(8306993735213931313)
XLA Ops:
  0.0 38.3 %shard_map.82 = (bf16[2,16,16,384]{3,2,1,0:T(8,128)(2,1)}, bf16[2,192,256]{2,1,0:T(8,128)(2,1)}) custom-call(bf16[2,3,192,384]{3,2,1,0:T(8,128)(2,1)} %retarded.1, bf16[2,2,192,384]{3,2,1,0:T(8,128)(2,1)} %injection.1, bf16[2,2,192,384]{3,2,1,0:T(8,128)(2,1)} %screened.1, s32[1,192]{1,0:T(1,128)} %bitcast.1, bf16[256,1536]{1,0:T(8,128)(2,1)} %constant.8.clone.tables, ...), custom_call_target="tpu_custom_call" | custom-call | tf_op jit(solution)/shard_map/pallas_call | solution.py:318
  38.3 0.0 copy-start
  38.3 1.0 %copy-done = bf16[2,16,16,384]{3,2,1,0:T(8,128)(2,1)S(1)} copy-done((bf16[2,16,16,384]{3,2,1,0:T(8,128)(2,1)S(1)}, bf16[2,16,16,384]{3,2,1,0:T(8,128)(2,1)}, u32[]{:S(2)}) %copy-start) | copy-done | bytes 393240
  39.3 0.0 copy-start.1
  39.3 0.9 %copy-done.1 = bf16[2,192,256]{2,1,0:T(8,128)(2,1)S(1)} copy-done((bf16[2,192,256]{2,1,0:T(8,128)(2,1)S(1)}, bf16[2,192,256]{2,1,0:T(8,128)(2,1)}, u32[]{:S(2)}) %copy-start.1) | copy-done | bytes 196632
  40.2 1.2 %shard_map.83 = bf16[2,2,192,384]{3,2,1,0:T(8,128)(2,1)} custom-call(bf16[2,16,16,384]{3,2,1,0:T(8,128)(2,1)S(1)} %copy-done, bf16[2,192,256]{2,1,0:T(8,128)(2,1)S(1)} %copy-done.1), custom_call_target="tpu_custom_call" | custom-call | tf_op jit(solution)/shard_map/pallas_call | solution.py:371
Async XLA Ops:
  38.3 1.0 %copy-start = (bf16[2,16,16,384]{3,2,1,0:T(8,128)(2,1)S(1)}, bf16[2,16,16,384]{3,2,1,0:T(8,128)(2,1)}, u32[]{:S(2)}) copy-start(bf16[2,16,16,384]{3,2,1,0:T(8,128)(2,1)} %get-tuple-element.7.back) | copy-start | bytes 1179652
  39.3 0.9 %copy-start.1 = (bf16[2,192,256]{2,1,0:T(8,128)(2,1)S(1)}, bf16[2,192,256]{2,1,0:T(8,128)(2,1)}, u32[]{:S(2)}) copy-start(bf16[2,192,256]{2,1,0:T(8,128)(2,1)} %get-tuple-element.8.places) | copy-start | bytes 589828

commit v3 on v2

--- a/solution.py
+++ b/solution.py
@@ -1,3 +1,4 @@
+import functools
 import math
 
 import jax
@@ -36,12 +37,13 @@
 
 
 def kernel(
-    retarded, injection, screened, pattern, tables, want_slot, want_col, want_row,
+    live, padded,
+    retarded, injection, screened, pattern, tables,
     back, places,
-    ret_v, inj_v, scr_v, pat_v, tab_v, slot_v, col_v, row_v,
+    ret_v, inj_v, scr_v, pat_v, tab_v,
     halo, row_wide, row_live, total, screen_hat,
-    places_v, s_send, s_recv, g_send, g_recv, c_send,
-    load_sem, halo_out, halo_in, s_out, s_in, g_out, g_in, c_out, c_in, own_sem, store_sem,
+    s_send, s_recv, g_send, g_recv, c_send,
+    load_sem, halo_out, halo_in, s_out, s_in, g_out, g_in, c_out, c_in, own_sem,
 ):
     owners = lax.axis_size("energy")
     slabs = lax.axis_size("slab")
@@ -55,18 +57,20 @@
     flat = owners * chunk
     count = owners * energies
 
+    share = -(-live // owners)
+    far, near = [owners // 2], []
+    while far[0] >> len(near) > 1:
+        near.append(far[0] >> len(near) + 1)
+
     loads = [
         pltpu.make_async_copy(source, target, load_sem.at[at])
         for at, (source, target) in enumerate(
             [
                 (pattern, pat_v),
-                (want_col, col_v),
                 (screened, scr_v),
-                (want_slot, slot_v),
                 (retarded, ret_v),
                 (injection, inj_v),
                 (tables, tab_v),
-                (want_row, row_v),
             ]
         )
     ]
@@ -90,9 +94,8 @@
     def _():
         pl.semaphore_signal(barrier, inc=1, device_id={"slab": slab + 1}, device_id_type=MESH)
 
-    def spread(source, target, out_sem, in_sem):
-        half = owners // 2
-        while half:
+    def spread(source, target, out_sem, in_sem, halves=None):
+        for half in halves or far + near:
             group = me // half
             first = (group + 1 - 2 * lax.rem(group, 2)) * half
 
@@ -109,7 +112,6 @@
                 return carry
 
             lax.fori_loop(0, half, send, 0)
-            half //= 2
 
     def wait_all(buffer, sem):
         rest = buffer.at[pl.ds(0, owners - 1)]
@@ -128,9 +130,15 @@
     def one_hot(left, right):
         return jnp.where(left == right, 1.0, 0.0).astype(BF16)
 
+    def wanted(shape, axis, size, energy):
+        at = lax.broadcasted_iota(jnp.int32, shape, axis).astype(F32)
+        owner = jnp.floor((at + 0.5) * (1.0 / size))
+        inside = at - owner * size - energy * padded
+        row = owner * share + inside
+        return jnp.where((inside >= 0) & (inside < share) & (row < live), row, -2.0)
+
+    picks = [one_hot(wanted((flat, 1), 0, chunk, e), key_row) for e in range(energies)]
     loads[1].wait()
-    picks = [one_hot(col_v[e], key_row) for e in range(energies)]
-    loads[2].wait()
     for kind in range(2):
         picked = sum(dot(picks[e], scr_v[e, kind]) for e in range(energies))
         s_send[:, kind] = picked.astype(BF16).reshape(owners, chunk, width)
@@ -161,8 +169,7 @@
     spread(s_send, s_recv, s_out, s_in)
     s_recv[me] = s_send[me]
 
-    loads[3].wait()
-    pick_rows = one_hot(slot_v[...], key_row)
+    pick_rows = one_hot(wanted((owners * padded, 1), 0, padded, 0), key_row)
 
     def widen(x):
         return times_i(x.astype(F32)).astype(BF16)
@@ -179,8 +186,8 @@
         left = dot(row_live[offset, e], expanded).astype(BF16)
         return dot_nt(left, row_wide[offset, e])
 
-    loads[4].wait()
-    loads[5].wait()
+    loads[2].wait()
+    loads[3].wait()
     prepare(1)
 
     @pl.when(has_left)
@@ -223,7 +230,6 @@
     factor = 1.0 / (count * math.sqrt(count))
 
     def convolve(kind):
-        wait_all(g_recv.at[kind], g_in.at[kind])
         green_hat = forward(g_recv[kind].reshape(flat, width))
         product = complex_times(green_hat, screen_hat[kind])
         turned = times_i(product)
@@ -232,24 +238,31 @@
         turned_low = (turned - turned_high.astype(F32)).astype(BF16)
         sigma = transform([turned_high, high, turned_high, high, turned_low, low])
         c_send[kind] = (sigma * factor).astype(BF16).reshape(owners, chunk, width)
-        spread(c_send.at[kind], back.at[kind], c_out.at[kind], c_in.at[kind])
+
+    def give_back(kind, halves):
+        spread(c_send.at[kind], back.at[kind], c_out.at[kind], c_in.at[kind], halves)
+
+    def keep_own(kind):
         own = pltpu.make_async_copy(c_send.at[kind, me], back.at[kind, me], own_sem.at[kind])
         own.start()
         return own
 
     green(0)
-    loads[6].wait()
+    loads[4].wait()
     wait_all(s_recv, s_in)
     for kind in range(2):
         screen_hat[kind] = forward(s_recv[:, kind].reshape(flat, width))
     green(1)
-    owns = [convolve(0), convolve(1)]
-
-    loads[7].wait()
+    wait_all(g_recv.at[0], g_in.at[0])
+    convolve(0)
+    give_back(0, near)
+    wait_all(g_recv.at[1], g_in.at[1])
+    give_back(0, far)
+    convolve(1)
+    give_back(1, far + near)
+    owns = [keep_own(0), keep_own(1)]
     for e in range(energies):
-        places_v[e] = one_hot(key_col, row_v[e])
-    store = pltpu.make_async_copy(places_v, places, store_sem)
-    store.start()
+        places[e] = one_hot(key_col, wanted((1, flat), 1, chunk, e))
 
     for kind in range(2):
         @pl.when(has_right)
@@ -266,7 +279,6 @@
         wait_all(c_send.at[kind], c_out.at[kind])
         wait_all(back.at[kind], c_in.at[kind])
         owns[kind].wait()
-    store.wait()
 
 
 def expand(back, places, result):
@@ -277,37 +289,25 @@
             result[e, kind] = dot(places[e], rows).astype(BF16)
 
 
-def layout(owners, energies, live):
-    share = -(-live // owners)
-    padded = -(-share // 8) * 8
-    while energies * padded % 16:
-        padded += 8
-    slot = np.arange(owners * padded)
-    wanted = slot // padded * share + slot % padded
-    wanted = np.where((slot % padded < share) & (wanted < live), wanted, -2)
-    by_energy = np.full((energies, owners, energies, padded), -2)
-    for e in range(energies):
-        by_energy[e, :, e] = wanted.reshape(owners, padded)
-    by_energy = by_energy.reshape(energies, -1)
-    count = owners * energies
+def transform_tables(count, padded):
     index = np.arange(count)
     angle = 2.0 * np.pi / count * (index[:, None] * index[None, :] % count)
-    tables = np.stack([np.cos(angle), np.sin(angle)]).astype(np.float32)
-    high = tables.astype(jnp.bfloat16)
-    low = (tables - high.astype(np.float32)).astype(jnp.bfloat16)
-    small = np.concatenate([high, low]).astype(np.float32)
+    tables = np.stack([np.cos(angle), -np.sin(angle)]).astype(np.float32)
+    high = tables.astype(jnp.bfloat16).astype(np.float32)
+    low = (tables - high).astype(jnp.bfloat16).astype(np.float32)
     eye = np.eye(padded, dtype=np.float32)
-    cos_high, sin_high, cos_low, sin_low = [np.kron(table, eye) for table in small]
-    wide = [cos_high, -sin_high, cos_low, -sin_low, cos_high, -sin_high]
-    wide = np.concatenate(wide, 1).astype(jnp.bfloat16)
-    return padded, wanted.astype(np.float32), by_energy.astype(np.float32), wide
+    wide = [np.kron(table, eye) for table in (*high, *low, *high)]
+    return np.concatenate(wide, 1).astype(jnp.bfloat16)
 
 
 def local(retarded, injection, screened, pattern):
     energies, _, block, width = retarded.shape
     owners = lax.axis_size("energy")
     live = block * 2 // 3
-    padded, wanted, by_energy, tables = layout(owners, energies, live)
+    padded = -(-live // (owners * 8)) * 8
+    while energies * padded % 16:
+        padded += 8
+    tables = transform_tables(owners * energies, padded)
     chunk = energies * padded
     flat = owners * chunk
     slots = owners * padded
@@ -316,34 +316,30 @@
     dma = pltpu.SemaphoreType.DMA
     blocks = (2, owners, chunk, width)
     back, places = pl.pallas_call(
-        kernel,
+        functools.partial(kernel, live, padded),
         out_shape=(
             jax.ShapeDtypeStruct(blocks, BF16),
             jax.ShapeDtypeStruct((energies, block, flat), BF16),
         ),
-        in_specs=[anywhere] * 8,
-        out_specs=(anywhere, anywhere),
+        in_specs=[anywhere] * 5,
+        out_specs=(vmem, vmem),
         scratch_shapes=[
             pltpu.VMEM(retarded.shape, BF16),
             pltpu.VMEM(injection.shape, BF16),
             pltpu.VMEM(screened.shape, BF16),
             pltpu.VMEM((1, block), pattern.dtype),
             pltpu.VMEM(tables.shape, BF16),
-            pltpu.VMEM((slots, 1), F32),
-            pltpu.VMEM((energies, flat, 1), F32),
-            pltpu.VMEM((energies, 1, flat), F32),
             pltpu.VMEM((2, 2, energies, block, width), BF16),
             pltpu.VMEM((3, energies, 2 * block, width), BF16),
             pltpu.VMEM((3, energies, slots, width), BF16),
             pltpu.VMEM((2, energies, slots, width), F32),
             pltpu.VMEM((2, flat, width), F32),
-            pltpu.VMEM((energies, block, flat), BF16),
             pltpu.VMEM((owners, 2, chunk, width), BF16),
             pltpu.VMEM((owners, 2, chunk, width), BF16),
             pltpu.VMEM(blocks, BF16),
             pltpu.VMEM(blocks, BF16),
             pltpu.VMEM(blocks, BF16),
-            dma((8,)),
+            dma((5,)),
             dma((2, 2)),
             dma((2, 2)),
             dma,
@@ -353,10 +349,9 @@
             dma((2,)),
             dma((2,)),
             dma((2,)),
-            dma,
         ],
         compiler_params=pltpu.CompilerParams(
-            collective_id=0, has_side_effects=True, vmem_limit_bytes=56 * 1024 * 1024
+            collective_id=0, has_side_effects=True, vmem_limit_bytes=53 * 1024 * 1024
         ),
     )(
         retarded,
@@ -364,9 +359,6 @@
         screened,
         pattern.reshape(1, -1),
         jnp.asarray(tables),
-        jnp.asarray(wanted.reshape(-1, 1)),
-        jnp.asarray(by_energy.reshape(energies, -1, 1)),
-        jnp.asarray(by_energy.reshape(energies, 1, -1)),
     )
     return pl.pallas_call(
         expand,

time: 41.6 us -> 41.1 us (0.988)
  local copies, waits for them, and re-layouts: 1.92 us -> 0.68 us
  Pallas kernels: 39.5 us -> 40.2 us
    unnamed x4 -> x2, local copies, waits for them, and re-layouts: 1.92 us -> 0.68 us
    pallas_call x1, Pallas kernels: 38.3 us -> 39 us  [local(): pl.pallas_call(functools.partial(kernel, live, padded), out_shape=(jax.Sh...]
where the time goes in v3:
time: 41.1 us; the launch traced here: 40.9 us
  Pallas kernels  40.2 us (98%)
  local copies, waits for them, and re-layouts  0.68 us (2%)
    pallas_call x1, Pallas kernels, local(): pl.pallas_call(functools.partial(kernel, live, padded), out_shape=(jax.Sh...  39 us
    pallas_call x1, Pallas kernels, local(): pl.pallas_call(expand, out_shape=jax.ShapeDtypeStruct(screened.shape, BF1...  1.18 us

profile of v3, /device:TPU:0, one launch (start us, length us, event | category | flops | bytes accessed | tf_op | source)
XLA Modules:
  0.0 40.9 jit_solution(14419895721611233826)
XLA Ops:
  0.0 0.0 copy-start
  0.0 0.7 %copy-done = s32[192]{0:T(256)S(1)} copy-done((s32[192]{0:T(256)S(1)}, s32[192]{0:T(256)}, u32[]{:S(2)}) %copy-start) | copy-done | bytes 792
  0.7 39.0 %shard_map.55 = (bf16[2,16,16,384]{3,2,1,0:T(8,128)(2,1)S(1)}, bf16[2,192,256]{2,1,0:T(8,128)(2,1)S(1)}) custom-call(bf16[2,3,192,384]{3,2,1,0:T(8,128)(2,1)} %retarded.1, bf16[2,2,192,384]{3,2,1,0:T(8,128)(2,1)} %injection.1, bf16[2,2,192,384]{3,2,1,0:T(8,128)(2,1)} %screened.1, s32[1,192]{1,0:T(1,128)S(1)} %bitcast.1, bf16[256,1536]{1,0:T(8,128)(2,1)} %constant.2.clone.tables), custom_call_target="tpu_custom_call" | custom-call | tf_op jit(solution)/shard_map/pallas_call | solution.py:318
  39.7 1.2 %shard_map.56 = bf16[2,2,192,384]{3,2,1,0:T(8,128)(2,1)} custom-call(bf16[2,16,16,384]{3,2,1,0:T(8,128)(2,1)S(1)} %get-tuple-element.7.back, bf16[2,192,256]{2,1,0:T(8,128)(2,1)S(1)} %get-tuple-element.8.places), custom_call_target="tpu_custom_call" | custom-call | tf_op jit(solution)/shard_map/pallas_call | solution.py:363
Async XLA Ops:
  0.0 0.7 %copy-start = (s32[192]{0:T(256)S(1)}, s32[192]{0:T(256)}, u32[]{:S(2)}) copy-start(s32[192]{0:T(256)} %param.8) | copy-start | bytes 2308

commit v4 on v3

--- a/solution.py
+++ b/solution.py
@@ -58,10 +58,6 @@
     count = owners * energies
 
     share = -(-live // owners)
-    far, near = [owners // 2], []
-    while far[0] >> len(near) > 1:
-        near.append(far[0] >> len(near) + 1)
-
     loads = [
         pltpu.make_async_copy(source, target, load_sem.at[at])
         for at, (source, target) in enumerate(
@@ -94,28 +90,55 @@
     def _():
         pl.semaphore_signal(barrier, inc=1, device_id={"slab": slab + 1}, device_id_type=MESH)
 
-    def spread(source, target, out_sem, in_sem, halves=None):
-        for half in halves or far + near:
-            group = me // half
-            first = (group + 1 - 2 * lax.rem(group, 2)) * half
-
-            def send(step, carry, half=half, first=first):
-                peer = first + lax.rem(me + step, half)
-                pltpu.make_async_remote_copy(
-                    src_ref=source.at[peer],
-                    dst_ref=target.at[me],
-                    send_sem=out_sem,
-                    recv_sem=in_sem,
-                    device_id={"energy": peer},
-                    device_id_type=MESH,
-                ).start()
-                return carry
-
-            lax.fori_loop(0, half, send, 0)
+    def spread(source, target, out_sem, in_sem):
+        half = owners // 2
+        mine = me // half * half
+
+        def send(peer):
+            pltpu.make_async_remote_copy(
+                src_ref=source.at[peer],
+                dst_ref=target.at[me],
+                send_sem=out_sem,
+                recv_sem=in_sem,
+                device_id={"energy": peer},
+                device_id_type=MESH,
+            ).start()
+
+        def pair(step, carry):
+            turn = lax.rem(me + step, half)
+            send(half - mine + turn)
+            send(mine + turn)
+            return carry
+
+        send(half - mine + lax.rem(me, half))
+        lax.fori_loop(1, half, pair, 0)
 
     def wait_all(buffer, sem):
         rest = buffer.at[pl.ds(0, owners - 1)]
         pltpu.make_async_copy(rest, rest, sem).wait()
+
+    pl.semaphore_wait(
+        barrier, owners - 1 + has_left.astype(jnp.int32) + has_right.astype(jnp.int32)
+    )
+
+    def halo_copy(side, kind):
+        return pltpu.make_async_remote_copy(
+            src_ref=injection.at[:, kind],
+            dst_ref=halo.at[side, kind],
+            send_sem=halo_out.at[side, kind],
+            recv_sem=halo_in.at[side, kind],
+            device_id={"slab": slab + 1 - 2 * side},
+            device_id_type=MESH,
+        )
+
+    for kind in range(2):
+        @pl.when(has_right)
+        def _():
+            halo_copy(0, kind).start()
+
+        @pl.when(has_left)
+        def _():
+            halo_copy(1, kind).start()
 
     loads[0].wait()
     pattern_row = pat_v[...].astype(F32)
@@ -143,29 +166,6 @@
         picked = sum(dot(picks[e], scr_v[e, kind]) for e in range(energies))
         s_send[:, kind] = picked.astype(BF16).reshape(owners, chunk, width)
 
-    pl.semaphore_wait(
-        barrier, owners - 1 + has_left.astype(jnp.int32) + has_right.astype(jnp.int32)
-    )
-
-    def halo_copy(side, kind):
-        return pltpu.make_async_remote_copy(
-            src_ref=injection.at[:, kind],
-            dst_ref=halo.at[side, kind],
-            send_sem=halo_out.at[side, kind],
-            recv_sem=halo_in.at[side, kind],
-            device_id={"slab": slab + 1 - 2 * side},
-            device_id_type=MESH,
-        )
-
-    for kind in range(2):
-        @pl.when(has_right)
-        def _():
-            halo_copy(0, kind).start()
-
-        @pl.when(has_left)
-        def _():
-            halo_copy(1, kind).start()
-
     spread(s_send, s_recv, s_out, s_in)
     s_recv[me] = s_send[me]
 
@@ -230,6 +230,7 @@
     factor = 1.0 / (count * math.sqrt(count))
 
     def convolve(kind):
+        wait_all(g_recv.at[kind], g_in.at[kind])
         green_hat = forward(g_recv[kind].reshape(flat, width))
         product = complex_times(green_hat, screen_hat[kind])
         turned = times_i(product)
@@ -238,9 +239,7 @@
         turned_low = (turned - turned_high.astype(F32)).astype(BF16)
         sigma = transform([turned_high, high, turned_high, high, turned_low, low])
         c_send[kind] = (sigma * factor).astype(BF16).reshape(owners, chunk, width)
-
-    def give_back(kind, halves):
-        spread(c_send.at[kind], back.at[kind], c_out.at[kind], c_in.at[kind], halves)
+        spread(c_send.at[kind], back.at[kind], c_out.at[kind], c_in.at[kind])
 
     def keep_own(kind):
         own = pltpu.make_async_copy(c_send.at[kind, me], back.at[kind, me], own_sem.at[kind])
@@ -253,13 +252,8 @@
     for kind in range(2):
         screen_hat[kind] = forward(s_recv[:, kind].reshape(flat, width))
     green(1)
-    wait_all(g_recv.at[0], g_in.at[0])
     convolve(0)
-    give_back(0, near)
-    wait_all(g_recv.at[1], g_in.at[1])
-    give_back(0, far)
     convolve(1)
-    give_back(1, far + near)
     owns = [keep_own(0), keep_own(1)]
     for e in range(energies):
         places[e] = one_hot(key_col, wanted((1, flat), 1, chunk, e))

time: 41.1 us -> 40.1 us (0.976)
  Pallas kernels: 40.2 us -> 39.3 us
    pallas_call x1, Pallas kernels: 39 us -> 38.1 us  [local(): pl.pallas_call(functools.partial(kernel, live, padded), out_shape=(jax.Sh...]
where the time goes in v4:
time: 40.1 us; the launch traced here: 40 us
  Pallas kernels  39.3 us (98%)
  local copies, waits for them, and re-layouts  0.68 us (2%)
    pallas_call x1, Pallas kernels, local(): pl.pallas_call(functools.partial(kernel, live, padded), out_shape=(jax.Sh...  38.1 us
    pallas_call x1, Pallas kernels, local(): pl.pallas_call(expand, out_shape=jax.ShapeDtypeStruct(screened.shape, BF1...  1.18 us

profile of v4, /device:TPU:0, one launch (start us, length us, event | category | flops | bytes accessed | tf_op | source)
XLA Modules:
  0.0 40.0 jit_solution(6164806040809652204)
XLA Ops:
  0.0 0.0 copy-start
  0.0 0.7 %copy-done = s32[192]{0:T(256)S(1)} copy-done((s32[192]{0:T(256)S(1)}, s32[192]{0:T(256)}, u32[]{:S(2)}) %copy-start) | copy-done | bytes 792
  0.7 38.1 %shard_map.55 = (bf16[2,16,16,384]{3,2,1,0:T(8,128)(2,1)S(1)}, bf16[2,192,256]{2,1,0:T(8,128)(2,1)S(1)}) custom-call(bf16[2,3,192,384]{3,2,1,0:T(8,128)(2,1)} %retarded.1, bf16[2,2,192,384]{3,2,1,0:T(8,128)(2,1)} %injection.1, bf16[2,2,192,384]{3,2,1,0:T(8,128)(2,1)} %screened.1, s32[1,192]{1,0:T(1,128)S(1)} %bitcast.1, bf16[256,1536]{1,0:T(8,128)(2,1)} %constant.2.clone.tables), custom_call_target="tpu_custom_call" | custom-call | tf_op jit(solution)/shard_map/pallas_call | solution.py:312
  38.8 1.2 %shard_map.56 = bf16[2,2,192,384]{3,2,1,0:T(8,128)(2,1)} custom-call(bf16[2,16,16,384]{3,2,1,0:T(8,128)(2,1)S(1)} %get-tuple-element.7.back, bf16[2,192,256]{2,1,0:T(8,128)(2,1)S(1)} %get-tuple-element.8.places), custom_call_target="tpu_custom_call" | custom-call | tf_op jit(solution)/shard_map/pallas_call | solution.py:357
Async XLA Ops:
  0.0 0.7 %copy-start = (s32[192]{0:T(256)S(1)}, s32[192]{0:T(256)}, u32[]{:S(2)}) copy-start(s32[192]{0:T(256)} %param.8) | copy-start | bytes 2308

commit v5 on v4

--- a/solution.py
+++ b/solution.py
@@ -91,10 +91,8 @@
         pl.semaphore_signal(barrier, inc=1, device_id={"slab": slab + 1}, device_id_type=MESH)
 
     def spread(source, target, out_sem, in_sem):
-        half = owners // 2
-        mine = me // half * half
-
-        def send(peer):
+        def send(step, carry):
+            peer = lax.rem(me + step, owners)
             pltpu.make_async_remote_copy(
                 src_ref=source.at[peer],
                 dst_ref=target.at[me],
@@ -103,15 +101,9 @@
                 device_id={"energy": peer},
                 device_id_type=MESH,
             ).start()
-
-        def pair(step, carry):
-            turn = lax.rem(me + step, half)
-            send(half - mine + turn)
-            send(mine + turn)
             return carry
 
-        send(half - mine + lax.rem(me, half))
-        lax.fori_loop(1, half, pair, 0)
+        lax.fori_loop(1, owners, send, 0)
 
     def wait_all(buffer, sem):
         rest = buffer.at[pl.ds(0, owners - 1)]
@@ -131,7 +123,7 @@
             device_id_type=MESH,
         )
 
-    for kind in range(2):
+    def send_halo(kind):
         @pl.when(has_right)
         def _():
             halo_copy(0, kind).start()
@@ -139,6 +131,17 @@
         @pl.when(has_left)
         def _():
             halo_copy(1, kind).start()
+
+    def take_halo(kind):
+        @pl.when(has_left)
+        def _():
+            halo_copy(0, kind).wait_recv()
+
+        @pl.when(has_right)
+        def _():
+            halo_copy(1, kind).wait_recv()
+
+    send_halo(0)
 
     loads[0].wait()
     pattern_row = pat_v[...].astype(F32)
@@ -205,13 +208,11 @@
     def green(kind):
         @pl.when(has_left)
         def _():
-            halo_copy(0, kind).wait_recv()
             for e in range(energies):
                 total[kind, e] += term(0, e, halo[0, kind, e])
 
         @pl.when(has_right)
         def _():
-            halo_copy(1, kind).wait_recv()
             for e in range(energies):
                 total[kind, e] += term(2, e, halo[1, kind, e])
 
@@ -246,11 +247,14 @@
         own.start()
         return own
 
+    take_halo(0)
+    send_halo(1)
     green(0)
     loads[4].wait()
     wait_all(s_recv, s_in)
     for kind in range(2):
         screen_hat[kind] = forward(s_recv[:, kind].reshape(flat, width))
+    take_halo(1)
     green(1)
     convolve(0)
     convolve(1)

time: 40.1 us -> 39.9 us (level)
  no operation moved by 1% of the time
where the time goes in v5:
time: 39.9 us; the launch traced here: 39.7 us
  Pallas kernels  39 us (98%)
  local copies, waits for them, and re-layouts  0.68 us (2%)
    pallas_call x1, Pallas kernels, local(): pl.pallas_call(functools.partial(kernel, live, padded), out_shape=(jax.Sh...  37.9 us
    pallas_call x1, Pallas kernels, local(): pl.pallas_call(expand, out_shape=jax.ShapeDtypeStruct(screened.shape, BF1...  1.18 us

profile of v5, /device:TPU:0, one launch (start us, length us, event | category | flops | bytes accessed | tf_op | source)
XLA Modules:
  0.0 39.7 jit_solution(3019390684600527569)
XLA Ops:
  0.0 0.0 copy-start
  0.0 0.7 %copy-done = s32[192]{0:T(256)S(1)} copy-done((s32[192]{0:T(256)S(1)}, s32[192]{0:T(256)}, u32[]{:S(2)}) %copy-start) | copy-done | bytes 792
  0.7 37.9 %shard_map.55 = (bf16[2,16,16,384]{3,2,1,0:T(8,128)(2,1)S(1)}, bf16[2,192,256]{2,1,0:T(8,128)(2,1)S(1)}) custom-call(bf16[2,3,192,384]{3,2,1,0:T(8,128)(2,1)} %retarded.1, bf16[2,2,192,384]{3,2,1,0:T(8,128)(2,1)} %injection.1, bf16[2,2,192,384]{3,2,1,0:T(8,128)(2,1)} %screened.1, s32[1,192]{1,0:T(1,128)S(1)} %bitcast.1, bf16[256,1536]{1,0:T(8,128)(2,1)} %constant.2.clone.tables), custom_call_target="tpu_custom_call" | custom-call | tf_op jit(solution)/shard_map/pallas_call | solution.py:316
  38.6 1.2 %shard_map.56 = bf16[2,2,192,384]{3,2,1,0:T(8,128)(2,1)} custom-call(bf16[2,16,16,384]{3,2,1,0:T(8,128)(2,1)S(1)} %get-tuple-element.7.back, bf16[2,192,256]{2,1,0:T(8,128)(2,1)S(1)} %get-tuple-element.8.places), custom_call_target="tpu_custom_call" | custom-call | tf_op jit(solution)/shard_map/pallas_call | solution.py:361
Async XLA Ops:
  0.0 0.7 %copy-start = (s32[192]{0:T(256)S(1)}, s32[192]{0:T(256)}, u32[]{:S(2)}) copy-start(s32[192]{0:T(256)} %param.8) | copy-start | bytes 2308

commit v6 on v5

--- a/solution.py
+++ b/solution.py
@@ -142,6 +142,7 @@
             halo_copy(1, kind).wait_recv()
 
     send_halo(0)
+    send_halo(1)
 
     loads[0].wait()
     pattern_row = pat_v[...].astype(F32)
@@ -248,7 +249,6 @@
         return own
 
     take_halo(0)
-    send_halo(1)
     green(0)
     loads[4].wait()
     wait_all(s_recv, s_in)

time: 39.9 us -> 37.1 us (0.930)
  Pallas kernels: 39 us -> 36.3 us
    pallas_call x1, Pallas kernels: 37.9 us -> 35.1 us  [local(): pl.pallas_call(functools.partial(kernel, live, padded), out_shape=(jax.Sh...]
where the time goes in v6:
time: 37.1 us; the launch traced here: 37 us
  Pallas kernels  36.3 us (98%)
  local copies, waits for them, and re-layouts  0.68 us (2%)
    pallas_call x1, Pallas kernels, local(): pl.pallas_call(functools.partial(kernel, live, padded), out_shape=(jax.Sh...  35.1 us
    pallas_call x1, Pallas kernels, local(): pl.pallas_call(expand, out_shape=jax.ShapeDtypeStruct(screened.shape, BF1...  1.18 us

profile of v6, /device:TPU:0, one launch (start us, length us, event | category | flops | bytes accessed | tf_op | source)
XLA Modules:
  0.0 37.0 jit_solution(15074117695027093086)
XLA Ops:
  0.0 0.0 copy-start
  0.0 0.7 %copy-done = s32[192]{0:T(256)S(1)} copy-done((s32[192]{0:T(256)S(1)}, s32[192]{0:T(256)}, u32[]{:S(2)}) %copy-start) | copy-done | bytes 792
  0.7 35.1 %shard_map.55 = (bf16[2,16,16,384]{3,2,1,0:T(8,128)(2,1)S(1)}, bf16[2,192,256]{2,1,0:T(8,128)(2,1)S(1)}) custom-call(bf16[2,3,192,384]{3,2,1,0:T(8,128)(2,1)} %retarded.1, bf16[2,2,192,384]{3,2,1,0:T(8,128)(2,1)} %injection.1, bf16[2,2,192,384]{3,2,1,0:T(8,128)(2,1)} %screened.1, s32[1,192]{1,0:T(1,128)S(1)} %bitcast.1, bf16[256,1536]{1,0:T(8,128)(2,1)} %constant.2.clone.tables), custom_call_target="tpu_custom_call" | custom-call | tf_op jit(solution)/shard_map/pallas_call | solution.py:316
  35.8 1.2 %shard_map.56 = bf16[2,2,192,384]{3,2,1,0:T(8,128)(2,1)} custom-call(bf16[2,16,16,384]{3,2,1,0:T(8,128)(2,1)S(1)} %get-tuple-element.7.back, bf16[2,192,256]{2,1,0:T(8,128)(2,1)S(1)} %get-tuple-element.8.places), custom_call_target="tpu_custom_call" | custom-call | tf_op jit(solution)/shard_map/pallas_call | solution.py:361
Async XLA Ops:
  0.0 0.7 %copy-start = (s32[192]{0:T(256)S(1)}, s32[192]{0:T(256)}, u32[]{:S(2)}) copy-start(s32[192]{0:T(256)} %param.8) | copy-start | bytes 2308

commit v7 on v6

--- a/solution.py
+++ b/solution.py
@@ -113,36 +113,25 @@
         barrier, owners - 1 + has_left.astype(jnp.int32) + has_right.astype(jnp.int32)
     )
 
-    def halo_copy(side, kind):
+    def halo_copy(side, kind, e):
         return pltpu.make_async_remote_copy(
-            src_ref=injection.at[:, kind],
-            dst_ref=halo.at[side, kind],
-            send_sem=halo_out.at[side, kind],
-            recv_sem=halo_in.at[side, kind],
+            src_ref=injection.at[e, kind],
+            dst_ref=halo.at[side, kind, e],
+            send_sem=halo_out.at[side, kind, e],
+            recv_sem=halo_in.at[side, kind, e],
             device_id={"slab": slab + 1 - 2 * side},
             device_id_type=MESH,
         )
 
-    def send_halo(kind):
+    pieces = [(kind, e) for kind in range(2) for e in range(energies)]
+    for piece in pieces:
         @pl.when(has_right)
         def _():
-            halo_copy(0, kind).start()
+            halo_copy(0, *piece).start()
 
         @pl.when(has_left)
         def _():
-            halo_copy(1, kind).start()
-
-    def take_halo(kind):
-        @pl.when(has_left)
-        def _():
-            halo_copy(0, kind).wait_recv()
-
-        @pl.when(has_right)
-        def _():
-            halo_copy(1, kind).wait_recv()
-
-    send_halo(0)
-    send_halo(1)
+            halo_copy(1, *piece).start()
 
     loads[0].wait()
     pattern_row = pat_v[...].astype(F32)
@@ -206,21 +195,28 @@
         for e in range(energies):
             total[kind, e] = term(1, e, inj_v[e, kind])
 
-    def green(kind):
+    def green(kind, e):
         @pl.when(has_left)
         def _():
-            for e in range(energies):
-                total[kind, e] += term(0, e, halo[0, kind, e])
+            halo_copy(0, kind, e).wait_recv()
+            total[kind, e] += term(0, e, halo[0, kind, e])
 
         @pl.when(has_right)
         def _():
-            for e in range(energies):
-                total[kind, e] += term(2, e, halo[1, kind, e])
-
-        parts = [total[kind, e].reshape(owners, per_energy, width) for e in range(energies)]
-        g_send[kind] = jnp.concatenate(parts, 1).astype(BF16)
-        spread(g_send.at[kind], g_recv.at[kind], g_out.at[kind], g_in.at[kind])
-        g_recv[kind, me] = g_send[kind, me]
+            halo_copy(1, kind, e).wait_recv()
+            total[kind, e] += term(2, e, halo[1, kind, e])
+
+        at = (kind, e)
+        g_send[kind, e] = total[kind, e].reshape(owners, per_energy, width).astype(BF16)
+        spread(g_send.at[at], g_recv.at[at], g_out.at[at], g_in.at[at])
+        g_recv[kind, e, me] = g_send[kind, e, me]
+
+    def green_rows(kind):
+        parts = []
+        for e in range(energies):
+            wait_all(g_recv.at[kind, e], g_in.at[kind, e])
+            parts.append(g_recv[kind, e].astype(F32))
+        return jnp.concatenate(parts, 1).reshape(flat, width).astype(BF16)
 
     def transform(pieces):
         return dot(tab_v[:, : flat * len(pieces)], jnp.concatenate(pieces, 0))
@@ -232,8 +228,7 @@
     factor = 1.0 / (count * math.sqrt(count))
 
     def convolve(kind):
-        wait_all(g_recv.at[kind], g_in.at[kind])
-        green_hat = forward(g_recv[kind].reshape(flat, width))
+        green_hat = forward(green_rows(kind))
         product = complex_times(green_hat, screen_hat[kind])
         turned = times_i(product)
         high, turned_high = product.astype(BF16), turned.astype(BF16)
@@ -248,32 +243,33 @@
         own.start()
         return own
 
-    take_halo(0)
-    green(0)
+    for e in range(energies):
+        green(0, e)
     loads[4].wait()
     wait_all(s_recv, s_in)
     for kind in range(2):
         screen_hat[kind] = forward(s_recv[:, kind].reshape(flat, width))
-    take_halo(1)
-    green(1)
+    for e in range(energies):
+        green(1, e)
     convolve(0)
     convolve(1)
     owns = [keep_own(0), keep_own(1)]
     for e in range(energies):
         places[e] = one_hot(key_col, wanted((1, flat), 1, chunk, e))
 
-    for kind in range(2):
+    for piece in pieces:
         @pl.when(has_right)
         def _():
-            halo_copy(0, kind).wait_send()
+            halo_copy(0, *piece).wait_send()
 
         @pl.when(has_left)
         def _():
-            halo_copy(1, kind).wait_send()
+            halo_copy(1, *piece).wait_send()
+
+        wait_all(g_send.at[piece], g_out.at[piece])
 
     wait_all(s_send, s_out)
     for kind in range(2):
-        wait_all(g_send.at[kind], g_out.at[kind])
         wait_all(c_send.at[kind], c_out.at[kind])
         wait_all(back.at[kind], c_in.at[kind])
         owns[kind].wait()
@@ -334,16 +330,16 @@
             pltpu.VMEM((2, flat, width), F32),
             pltpu.VMEM((owners, 2, chunk, width), BF16),
             pltpu.VMEM((owners, 2, chunk, width), BF16),
-            pltpu.VMEM(blocks, BF16),
-            pltpu.VMEM(blocks, BF16),
+            pltpu.VMEM((2, energies, owners, padded, width), BF16),
+            pltpu.VMEM((2, energies, owners, padded, width), BF16),
             pltpu.VMEM(blocks, BF16),
             dma((5,)),
-            dma((2, 2)),
-            dma((2, 2)),
+            dma((2, 2, energies)),
+            dma((2, 2, energies)),
             dma,
             dma,
-            dma((2,)),
-            dma((2,)),
+            dma((2, energies)),
+            dma((2, energies)),
             dma((2,)),
             dma((2,)),
             dma((2,)),

time: 37.1 us -> 34.7 us (0.935)
  Pallas kernels: 36.3 us -> 33.9 us
    pallas_call x1, Pallas kernels: 35.1 us -> 32.7 us  [local(): pl.pallas_call(functools.partial(kernel, live, padded), out_shape=(jax.Sh...]
where the time goes in v7:
time: 34.7 us; the launch traced here: 34.6 us
  Pallas kernels  33.9 us (98%)
  local copies, waits for them, and re-layouts  0.68 us (2%)
    pallas_call x1, Pallas kernels, local(): pl.pallas_call(functools.partial(kernel, live, padded), out_shape=(jax.Sh...  32.7 us
    pallas_call x1, Pallas kernels, local(): pl.pallas_call(expand, out_shape=jax.ShapeDtypeStruct(screened.shape, BF1...  1.18 us

profile of v7, /device:TPU:0, one launch (start us, length us, event | category | flops | bytes accessed | tf_op | source)
XLA Modules:
  0.0 34.6 jit_solution(12497076452803529848)
XLA Ops:
  0.0 0.0 copy-start
  0.0 0.7 %copy-done = s32[192]{0:T(256)S(1)} copy-done((s32[192]{0:T(256)S(1)}, s32[192]{0:T(256)}, u32[]{:S(2)}) %copy-start) | copy-done | bytes 792
  0.7 32.7 %shard_map.55 = (bf16[2,16,16,384]{3,2,1,0:T(8,128)(2,1)S(1)}, bf16[2,192,256]{2,1,0:T(8,128)(2,1)S(1)}) custom-call(bf16[2,3,192,384]{3,2,1,0:T(8,128)(2,1)} %retarded.1, bf16[2,2,192,384]{3,2,1,0:T(8,128)(2,1)} %injection.1, bf16[2,2,192,384]{3,2,1,0:T(8,128)(2,1)} %screened.1, s32[1,192]{1,0:T(1,128)S(1)} %bitcast.1, bf16[256,1536]{1,0:T(8,128)(2,1)} %constant.2.clone.tables), custom_call_target="tpu_custom_call" | custom-call | tf_op jit(solution)/shard_map/pallas_call | solution.py:312
  33.4 1.2 %shard_map.56 = bf16[2,2,192,384]{3,2,1,0:T(8,128)(2,1)} custom-call(bf16[2,16,16,384]{3,2,1,0:T(8,128)(2,1)S(1)} %get-tuple-element.7.back, bf16[2,192,256]{2,1,0:T(8,128)(2,1)S(1)} %get-tuple-element.8.places), custom_call_target="tpu_custom_call" | custom-call | tf_op jit(solution)/shard_map/pallas_call | solution.py:357
Async XLA Ops:
  0.0 0.7 %copy-start = (s32[192]{0:T(256)S(1)}, s32[192]{0:T(256)}, u32[]{:S(2)}) copy-start(s32[192]{0:T(256)} %param.8) | copy-start | bytes 2308

commit v8 on v7

--- a/solution.py
+++ b/solution.py
@@ -249,9 +249,10 @@
     wait_all(s_recv, s_in)
     for kind in range(2):
         screen_hat[kind] = forward(s_recv[:, kind].reshape(flat, width))
-    for e in range(energies):
+    for e in range(energies - 1):
         green(1, e)
     convolve(0)
+    green(1, energies - 1)
     convolve(1)
     owns = [keep_own(0), keep_own(1)]
     for e in range(energies):

time: 34.7 us -> 39.8 us (1.15)
  Pallas kernels: 33.9 us -> 38.9 us
    pallas_call x1, Pallas kernels: 32.7 us -> 37.7 us  [local(): pl.pallas_call(functools.partial(kernel, live, padded), out_shape=(jax.Sh...]
where the time goes in v8:
time: 39.8 us; the launch traced here: 39.6 us
  Pallas kernels  38.9 us (98%)
  local copies, waits for them, and re-layouts  0.68 us (2%)
    pallas_call x1, Pallas kernels, local(): pl.pallas_call(functools.partial(kernel, live, padded), out_shape=(jax.Sh...  37.7 us
    pallas_call x1, Pallas kernels, local(): pl.pallas_call(expand, out_shape=jax.ShapeDtypeStruct(screened.shape, BF1...  1.18 us

profile of v8, /device:TPU:0, one launch (start us, length us, event | category | flops | bytes accessed | tf_op | source)
XLA Modules:
  0.0 39.6 jit_solution(14109147048779997385)
XLA Ops:
  0.0 0.0 copy-start
  0.0 0.7 %copy-done = s32[192]{0:T(256)S(1)} copy-done((s32[192]{0:T(256)S(1)}, s32[192]{0:T(256)}, u32[]{:S(2)}) %copy-start) | copy-done | bytes 792
  0.7 37.7 %shard_map.55 = (bf16[2,16,16,384]{3,2,1,0:T(8,128)(2,1)S(1)}, bf16[2,192,256]{2,1,0:T(8,128)(2,1)S(1)}) custom-call(bf16[2,3,192,384]{3,2,1,0:T(8,128)(2,1)} %retarded.1, bf16[2,2,192,384]{3,2,1,0:T(8,128)(2,1)} %injection.1, bf16[2,2,192,384]{3,2,1,0:T(8,128)(2,1)} %screened.1, s32[1,192]{1,0:T(1,128)S(1)} %bitcast.1, bf16[256,1536]{1,0:T(8,128)(2,1)} %constant.2.clone.tables), custom_call_target="tpu_custom_call" | custom-call | tf_op jit(solution)/shard_map/pallas_call | solution.py:313
  38.4 1.2 %shard_map.56 = bf16[2,2,192,384]{3,2,1,0:T(8,128)(2,1)} custom-call(bf16[2,16,16,384]{3,2,1,0:T(8,128)(2,1)S(1)} %get-tuple-element.7.back, bf16[2,192,256]{2,1,0:T(8,128)(2,1)S(1)} %get-tuple-element.8.places), custom_call_target="tpu_custom_call" | custom-call | tf_op jit(solution)/shard_map/pallas_call | solution.py:358
Async XLA Ops:
  0.0 0.7 %copy-start = (s32[192]{0:T(256)S(1)}, s32[192]{0:T(256)}, u32[]{:S(2)}) copy-start(s32[192]{0:T(256)} %param.8) | copy-start | bytes 2308
